TPU v7x, 512 devices: a whole 4x4x16 slice. The times are simulated.
512 devices in a mesh: dp: 128 (over x, z_lo, y, core), mp: 4 (over z_hi).
Axes of the slice: x: 4, y: 4, z: 16 (z_hi: 4, z_lo: 4; z = z_hi * 4 + z_lo), core: 2. Of those that a mesh axis runs over, the one named last changes fastest.
Arguments:
- query_embedding_cache: bfloat16 [128, 4096], P('dp'), may hold values from -0.1 to 0.1
- passage_embedding_cache: bfloat16 [128, 4096], P('dp'), may hold values from -0.099609375 to 0.099609375
- positive: int32 [128], P('dp'), may hold values from 0 to 127, as said below
- attention_head_outputs: bfloat16 [65536, 4096], P('dp', 'mp'), may hold values from -6 to 6
- residual: bfloat16 [65536, 4096], P('dp', 'mp'), may hold values from -16 to 16
- output_projection_weight: bfloat16 [4096, 4096], P('dp', 'mp'), may hold values from -0.375 to 0.375
- final_norm_gain: float32 [4096], P('mp'), may hold values from 0.1 to 1.9
- adapter_down_weight: bfloat16 [16, 4096], replicated, may hold values from -0.09375 to 0.09375
- adapter_up_weight: bfloat16 [16, 4096], P(None, 'mp'), may hold values from -1.5 to 1.5
- sequence_length: int32 [128], P('dp'), may hold values from 64 to 512
Outputs:
- query_grad: float32 [128, 4096], P('dp')
- passage_grad: float32 [128, 4096], P('dp')
- down_grad: float32 [16, 4096], P(None, ('mp', 'dp'))
- up_grad: float32 [16, 4096], P(None, ('mp', 'dp'))
Inputs may be any that keep to these rules, and one draw needn't show every extreme that they name: Each passage is the positive of exactly one query.
All inputs are finite; a program needn't handle non-finite values.
Results may differ from a plain program's by a relative error of at most 0.0009.
The roundings to bfloat16 on the way count: a program that leaves them out, or rounds other values in their place, can miss the bound.
Values may be sent and summed in bfloat16 or wider, within the bound.
No kernel may reach another device: no remote copies, remote signals or barrier semaphores. Data moves between devices by JAX's collectives and lax.ppermute only.
A program may use at most 64 MiB of HBM per device.

v0:
```python
import jax
import jax.numpy as jnp
from jax import lax
from jax.sharding import PartitionSpec as P

logit_divisor = 0.02
unit_floor = 1e-06
norm_floor = 1e-05


def unit_rows(rows):
    wide = rows.astype(jnp.float32)
    scale = lax.rsqrt(jnp.sum(wide * wide, axis=1, keepdims=True) + unit_floor)
    return (wide * scale, scale)


def pairwise_similarity_tile(left, right):
    return lax.dot_general(
        left, right, (((1,), (1,)), ((), ())), preferred_element_type=jnp.float32
    )


def cross_cols(left, right):
    return lax.dot_general(
        left, right, (((0,), (0,)), ((), ())), preferred_element_type=jnp.float32
    )


def shards(
    query_embedding_cache,
    passage_embedding_cache,
    positive,
    attention_head_outputs,
    residual,
    output_projection_weight,
    final_norm_gain,
    adapter_down_weight,
    adapter_up_weight,
    sequence_length,
):
    pair_rows = query_embedding_cache.shape[0]
    my_base = lax.axis_index("dp") * pair_rows
    head_outputs = lax.all_gather(attention_head_outputs, "mp", axis=1, tiled=True)
    local_cols = output_projection_weight.shape[1]
    projected_output = jnp.dot(
        head_outputs,
        lax.all_gather(output_projection_weight, "dp", axis=0, tiled=True),
        preferred_element_type=jnp.float32,
    )
    lowrank_input = pairwise_similarity_tile(head_outputs, adapter_down_weight)
    lowrank_input_half = lowrank_input.astype(jnp.bfloat16)
    hidden_state = (
        residual.astype(jnp.float32)
        + projected_output
        + 2.0 * jnp.dot(lowrank_input_half, adapter_up_weight, preferred_element_type=jnp.float32)
    )
    sumsq_part = jnp.sum(hidden_state * hidden_state, axis=1)
    query_unit, query_scale = unit_rows(query_embedding_cache)
    passage_unit, passage_scale = unit_rows(passage_embedding_cache)
    question_portion = query_unit.astype(jnp.bfloat16)
    document_portion = passage_unit.astype(jnp.bfloat16)
    document_vectors = lax.all_gather(document_portion, "dp", axis=0, tiled=True)
    similarity_table = pairwise_similarity_tile(question_portion, document_vectors) / logit_divisor
    partition_function = jnp.log(jnp.sum(jnp.exp(similarity_table), axis=1))
    column_ids = lax.broadcasted_iota(jnp.int32, similarity_table.shape, 1)
    positive_label = (column_ids == positive[:, None]).astype(jnp.float32)
    normalized_probability = (
        (jnp.exp(similarity_table - partition_function[:, None]) - positive_label) / logit_divisor
    ).astype(jnp.bfloat16)
    query_dir = jnp.dot(
        normalized_probability, document_vectors, preferred_element_type=jnp.float32
    )
    question_vectors, every_row_total, all_positive = (
        lax.all_gather(question_portion.astype(jnp.float32), "dp", axis=0, tiled=True).astype(
            question_portion.dtype
        ),
        lax.all_gather(partition_function, "dp", axis=0, tiled=True),
        lax.all_gather(positive, "dp", axis=0, tiled=True),
    )
    similarity_by_candidate = (
        pairwise_similarity_tile(question_vectors, document_portion) / logit_divisor
    )
    own_ids = my_base + lax.broadcasted_iota(jnp.int32, similarity_by_candidate.shape, 1)
    column_target_ids = (all_positive[:, None] == own_ids).astype(jnp.float32)
    column_softmax_weight = (
        (jnp.exp(similarity_by_candidate - every_row_total[:, None]) - column_target_ids)
        / logit_divisor
    ).astype(jnp.bfloat16)
    passage_dir = cross_cols(column_softmax_weight, question_vectors)
    query_grad = (
        query_dir - query_unit * jnp.sum(query_unit * query_dir, axis=1, keepdims=True)
    ) * query_scale
    passage_grad = (
        passage_dir - passage_unit * jnp.sum(passage_unit * passage_dir, axis=1, keepdims=True)
    ) * passage_scale
    upper = lax.dynamic_slice_in_dim(
        passage_grad[0], lax.axis_index("mp") * local_cols, local_cols, 0
    )
    scaled = final_norm_gain * upper
    width = head_outputs.shape[1]
    seq_rows = hidden_state.shape[0]
    length = sequence_length[0]
    positions = lax.broadcasted_iota(jnp.int32, (seq_rows,), 0)
    mask = (positions < length).astype(jnp.float32) / length.astype(jnp.float32)
    up_weight_wide = adapter_up_weight.astype(jnp.float32)
    dot_part = jnp.dot(hidden_state, scaled, precision=lax.Precision.HIGHEST)
    sumsq = lax.psum(sumsq_part, "mp")
    inverse = lax.rsqrt(sumsq / width + norm_floor)
    dot_row = lax.psum(dot_part, "mp")
    factor = inverse**3 * dot_row / width
    hidden_grad = mask[:, None] * (
        scaled[None, :] * inverse[:, None] - hidden_state * factor[:, None]
    )
    low_part = jnp.dot(hidden_grad, up_weight_wide.T, precision=lax.Precision.HIGHEST)
    low_grad = 2.0 * lax.psum(low_part, "mp")
    low_grad_bf = low_grad.astype(jnp.bfloat16)
    down_term = cross_cols(low_grad_bf, attention_head_outputs)
    up_term = 2.0 * lax.dot_general(
        lowrank_input_half.astype(jnp.float32),
        hidden_grad,
        (((0,), (0,)), ((), ())),
        precision=lax.Precision.HIGHEST,
    )
    down_grad, up_grad = (
        lax.psum_scatter(down_term, "dp", scatter_dimension=1, tiled=True),
        lax.psum_scatter(up_term, "dp", scatter_dimension=1, tiled=True),
    )
    return (query_grad, passage_grad, down_grad, up_grad)


def solution(mesh):
    placed = (
        P("dp", None),
        P("dp", None),
        P("dp"),
        P("dp", "mp"),
        P("dp", "mp"),
        P("dp", "mp"),
        P("mp"),
        P(),
        P(None, "mp"),
        P("dp"),
    )
    return jax.shard_map(
        shards,
        mesh=mesh,
        in_specs=placed,
        out_specs=(P("dp", None), P("dp", None), P(None, ("mp", "dp")), P(None, ("mp", "dp"))),
        check_vma=False,
    )
```

profile of v0, /device:TPU:1, one launch (start us, length us, event | category | flops | bytes accessed | tf_op | source)
XLA Modules:
  0.0 2165.2 jit_solution(16886595677051509566)
XLA Ops:
  7.3 1.4 multiply_reduce_fusion.3
  9.3 1.3 convert_bitcast_fusion
  11.4 1.4 multiply_reduce_fusion.4
  13.5 204.7 %all-gather.11.cloned.1.call-done = bf16[128,1,4096]{2,1,0:T(2,128)(2,1)} async-done(((bf16[1,1,4096]{2,1,0:T(2,128)(2,1)}), bf16[128,1,4096]{2,1,0:T(2,128)(2,1)}) %all-gather.11.cloned.1.call-update) | async-done | bytes 1048592 | tf_op jit(solution)/shard_map/all_gather | solution.py:62
  218.2 3.4 exponential_reduce_fusion
  222.3 2.8 fusion.12
  225.1 1.3 bitcast_convert_fusion
  229.8 0.8 dynamic-update-slice.1
  230.6 15.6 all-reduce.1
  247.0 403.7 %all-reduce = f32[128]{0:T(128)S(1)} all-reduce(f32[128]{0:T(128)S(1)} %dynamic-update-slice), channel_id=1, replica_groups=mesh['dp'=128,'mp'=4] {'dp'}, use_global_device_ids=true, to_apply=%add | all-reduce | flops 128 | bytes 1024
  650.7 5.2 multiply_reduce_fusion.1
  656.7 3.4 convolution_convert_fusion
  660.1 139.4 %all-gather.9.cloned.1.call-done = bf16[4096,1024]{1,0:T(8,128)(2,1)} async-done(((bf16[32,1024]{1,0:T(8,128)(2,1)}), bf16[4096,1024]{1,0:T(8,128)(2,1)}) %all-gather.9.cloned.1.call-update) | async-done | bytes 8388624 | tf_op jit(solution)/shard_map/all_gather | solution.py:47
  799.5 8.1 fusion.59
  808.3 1.9 fusion.60
  810.2 14.3 all-reduce.5
  824.5 1.4 fusion.1
  825.9 2.9 fusion.2
  828.8 20.2 psum.23
  849.0 1.4 fusion.28
  850.4 1.3 subtract_multiply_fusion.6
  851.7 1304.4 %all-reduce.8.cloned.1.call-done = (f32[16,1024]{0,1:T(8,128)}, f32[16,1024]{0,1:T(8,128)}) async-done(((f32[16,1024]{0,1:T(8,128)}, f32[16,1024]{0,1:T(8,128)}), (f32[16,1024]{0,1:T(8,128)}, f32[16,1024]{0,1:T(8,128)})) %all-reduce.8.cloned.1.call-update) | async-done | bytes 131088
  2156.1 1.3 constant_dynamic-slice_fusion.1
  2157.4 1.3 constant_dynamic-slice_fusion
  (39 shorter events, 4.4 us)
Async XLA Ops:
  7.2 649.5 %copy-start = (bf16[16,4096]{1,0:T(8,128)(2,1)S(1)}, bf16[16,4096]{1,0:T(8,128)(2,1)}, u32[]{:S(2)}) copy-start(bf16[16,4096]{1,0:T(8,128)(2,1)} %param.17) | copy-start | bytes 393220
  7.2 221.3 %copy-start.8 = (u32[512]{0:T(512)S(1)}, u32[512]{0:T(512)}, u32[]{:S(2)}) copy-start(u32[512]{0:T(512)} %constant.49) | copy-start | bytes 6148
  7.2 643.5 %copy-start.4 = (bf16[1,4096]{1,0:T(2,128)(2,1)S(1)}, bf16[1,4096]{1,0:T(2,128)(2,1)}, u32[]{:S(2)}) copy-start(bf16[1,4096]{1,0:T(2,128)(2,1)} %param.11) | copy-start | bytes 24580
  7.2 217.9 %copy-start.3 = (bf16[1,4096]{1,0:T(2,128)(2,1)S(1)}, bf16[1,4096]{1,0:T(2,128)(2,1)}, u32[]{:S(2)}) copy-start(bf16[1,4096]{1,0:T(2,128)(2,1)} %param.10) | copy-start | bytes 24580
  7.2 210.9 %all-gather.11.cloned.1.call-start = ((), (), s32[]{:S(2)}) async-start(), calls=%async_computation.2 | async-start | bytes 2113536 | tf_op jit(solution)/shard_map/all_gather | solution.py:62
  10.7 640.0 %all-gather.13.cloned.1.call-start = ((), (), s32[]{:S(2)}) async-start(), calls=%async_computation.3 | async-start | bytes 2113536 | tf_op jit(solution)/shard_map/all_gather | solution.py:74
  225.1 431.5 %copy-start.7 = (f32[1024]{0:T(1024)S(1)}, f32[1024]{0:T(1024)}, u32[]{:S(2)}) copy-start(f32[1024]{0:T(1024)} %param.16) | copy-start | bytes 12292
  226.4 430.2 %all-gather.7.cloned.1.call-start = ((), (), s32[]{:S(2)}) async-start(), calls=%async_computation | async-start | bytes 5242880 | tf_op jit(solution)/shard_map/all_gather | solution.py:43
  227.1 572.3 %all-gather.9.cloned.1.call-start = ((), (), s32[]{:S(2)}) async-start(), calls=%async_computation.1 | async-start | bytes 8454144 | tf_op jit(solution)/shard_map/all_gather | solution.py:47
  227.7 1928.4 %all-reduce.8.cloned.1.call-start = ((), (), s32[]{:S(2)}) async-start(), calls=%async_computation.4 | async-start | bytes 2097152
  656.6 3.5 copy-start.6
  660.1 147.6 %copy-start.2 = (bf16[512,1024]{1,0:T(8,128)(2,1)S(1)}, bf16[512,1024]{1,0:T(8,128)(2,1)}, u32[]{:S(2)}) copy-start(bf16[512,1024]{1,0:T(8,128)(2,1)} %param.14) | copy-start | bytes 3145732
  660.1 147.6 %copy-start.5 = (bf16[16,1024]{1,0:T(8,128)(2,1)S(1)}, bf16[16,1024]{1,0:T(8,128)(2,1)}, u32[]{:S(2)}) copy-start(bf16[16,1024]{1,0:T(8,128)(2,1)} %param.18) | copy-start | bytes 98308
  825.9 23.1 %copy-start.1 = (bf16[512,1024]{1,0:T(8,128)(2,1)S(1)}, bf16[512,1024]{1,0:T(8,128)(2,1)}, u32[]{:S(2)}) copy-start(bf16[512,1024]{1,0:T(8,128)(2,1)} %param.13) | copy-start | bytes 3145732
Sparse Core Ops, SparseCore 0:
  10.8 207.2 all-gather.10
  226.5 200.1 all-gather.12
  428.8 160.0 all-gather.6
  590.9 208.5 all-gather.8
  850.5 1305.5 all-reduce.7
where the time goes:
time: 2170 us
  waiting for transfers between devices  1650 us (76%)
  blocking collectives  454 us (21%)
  matrix products  31.2 us (1%)
    unnamed x6, waiting for transfers between devices  1310 us
    unnamed x2, blocking collectives  419 us
    all_gather x1, waiting for transfers between devices, shards(): lax.all_gather(document_portion, 'dp', axis=0, tiled=True)  205 us
    all_gather x1, waiting for transfers between devices, shards(): lax.all_gather(output_projection_weight, 'dp', axis=0, tiled=True)  139 us
  transfers between devices with their start and end apart: 5, of which 3 were waited for; matrix products, arithmetic and copies ran while one was open for 1% of the time, Pallas kernels for 0%

commit v1 on v0

v1 whole, which is shorter than its diff:
```python
import jax
import jax.numpy as jnp
from jax import lax
from jax.experimental import pallas as pl
from jax.experimental.pallas import tpu as pltpu
from jax.sharding import Mesh, PartitionSpec as P

logit_divisor = 0.02
unit_floor = 1e-06
norm_floor = 1e-05
AXES = ("x", "zl", "y", "core", "mp")
SIZES = (4, 4, 4, 2, 4)
DP = AXES[:4]
f32 = jnp.float32
bf16 = jnp.bfloat16


def ring(step):
    return [(i, (i + step) % 4) for i in range(4)]


def dot(left, right, dims, precision=None):
    return lax.dot_general(
        left, right, (dims, ((), ())), precision=precision, preferred_element_type=f32
    )


def gather(rows, axes):
    return lax.all_gather(rows, axes, axis=0, tiled=True)


def spread(rows, axis, size):
    copies = jnp.broadcast_to(rows[None], (size,) + rows.shape)
    return lax.all_to_all(copies, axis, 0, 0, tiled=True).reshape(-1, rows.shape[1])


def unit_rows(rows):
    wide = rows.astype(f32)
    scale = lax.rsqrt(jnp.sum(wide * wide, axis=1, keepdims=True) + unit_floor)
    return (wide * scale, scale)


def gather_line(weight, query, passage, positive):
    tail = jnp.concatenate(
        [
            query.reshape(8, 512),
            passage.reshape(8, 512),
            jnp.broadcast_to(positive.astype(bf16)[:, None], (2, 512)),
        ]
    )
    parts = [jnp.concatenate([weight[:, :512], tail]), jnp.concatenate([weight[:, 512:], tail])]
    sent = jnp.stack(parts * 4)
    line = lax.all_to_all(sent, ("zl", "core"), 0, 0, tiled=True)
    pairs = jnp.concatenate([line[:, 32:48].reshape(8, 8192), line[:, 48, :128]], axis=1)
    return line[:, :32].reshape(4, 64, 512), pairs


def pair_grads(query, passage, packed):
    queries, passages = packed[:, :4096], packed[:, 4096:8192]
    targets = packed[:, 8192:8193].astype(f32)
    place = lax.broadcasted_iota(jnp.int32, (1, 128), 1)
    x, y, zl, core = place // 32, (place // 8) % 4, (place // 2) % 4, place % 2
    ids = (((x * 4 + zl) * 4 + y) * 2 + core).astype(f32)
    query_unit, _ = unit_rows(queries)
    passage_unit, _ = unit_rows(passages)
    query_bf, passage_bf = query_unit.astype(bf16), passage_unit.astype(bf16)
    scores = dot(query_bf, passage_bf, ((1,), (1,))) / logit_divisor
    row_total = jnp.log(jnp.sum(jnp.exp(scores), axis=1, keepdims=True))
    label = (targets == ids).astype(f32)
    weights = ((jnp.exp(scores - row_total) - label) / logit_divisor).astype(bf16)
    me = lax.axis_index(("x", "y", "zl", "core"))
    own_row = lax.dynamic_slice_in_dim(weights, me, 1, 0)
    own_col = jnp.sum(
        jnp.where(place == me, weights.astype(f32), 0.0), axis=1, keepdims=True
    ).astype(bf16)
    query_dir = dot(own_row, passage_bf, ((1,), (0,)))
    passage_dir = dot(own_col, query_bf, ((0,), (0,)))

    def project(rows, direction):
        unit, scale = unit_rows(rows)
        return (direction - unit * jnp.sum(unit * direction, axis=1, keepdims=True)) * scale

    return project(query, query_dir), project(passage, passage_dir)


def gather_near(part):
    return lax.ppermute(part, "mp", ring(1)), lax.ppermute(part, "mp", ring(3))


def gather_far(before, after):
    cut = before.shape[0] // 2
    left = lax.ppermute(before[:cut], "mp", ring(1))
    right = lax.ppermute(after[cut:], "mp", ring(3))
    return jnp.stack([before, after, jnp.concatenate([left, right])])


def gather_valid(part, count):
    tokens, cols = part.shape

    def prefix(size):
        def branch(rows):
            if size == 0:
                return jnp.zeros((3, tokens, cols), rows.dtype)
            blocks = gather_far(*gather_near(rows[:size]))
            return jnp.pad(blocks, ((0, 0), (0, tokens - size), (0, 0)))

        return branch

    return lax.switch(count, [prefix(size) for size in range(0, tokens + 1, 64)], part)


def split(values):
    high = values.astype(bf16)
    return high, (values - high.astype(f32)).astype(bf16)


def hidden_kernel(
    place_ref, heads_ref, first_ref, second_ref, own_ref, other_ref, resid_ref, down_ref, up_ref,
    rows_ref, hidden_ref, low_ref, stats_ref, heads, weights, stats, sems
):
    mp, core = place_ref[0], place_ref[1]
    tokens, cols = heads_ref.shape
    cut = first_ref.shape[1]
    copies = []
    for i in range(4):
        at = pl.ds(pl.multiple_of(lax.rem(mp + (0, 3, 1, 2)[i], 4) * cols, cols), cols)
        if i == 0:
            copies.append(pltpu.make_async_copy(heads_ref, heads.at[:, at], sems.at[4]))
            continue
        for k, ref in enumerate((first_ref, second_ref)):
            part = heads.at[pl.ds(k * cut, cut), at]
            copies.append(pltpu.make_async_copy(ref.at[i - 1], part, sems.at[3 + 2 * i + k]))
    early = len(copies)
    for i in range(4):
        ref = own_ref if i < 2 else other_ref
        part = ref.at[:, :, :, pl.ds((i % 2) * 256, 256)]
        copies.append(pltpu.make_async_copy(part, weights.at[i], sems.at[i]))
    for copy in copies:
        copy.start()
    for copy in copies[:early]:
        copy.wait()

    low = dot(down_ref[...], heads[...], ((1,), (1,)))
    low_bf = low.astype(bf16)
    low_ref[...] = low_bf
    stats[...] = jnp.zeros_like(stats)

    @pl.loop(0, 4)
    def _(step):
        pltpu.make_async_copy(weights.at[step], weights.at[step], sems.at[step]).wait()
        half = jnp.where(step < 2, core, 1 - core)
        at = pl.multiple_of(half * 512 + lax.rem(step, 2) * 256, 256)
        columns = pl.ds(at, 256)
        total = resid_ref[:, columns].astype(f32) + 2.0 * dot(
            low_bf, up_ref[:, columns], ((0,), (0,))
        )
        rows = jnp.concatenate(
            [
                weights[step, x * 4 + y, zl]
                for x in range(4)
                for zl in range(4)
                for y in range(4)
            ]
        )
        proj = dot(heads[...], rows, ((1,), (0,)))
        total += proj
        hidden_ref[:, columns] = total
        high, rest = split(total)
        row_high, row_rest = split(rows_ref[columns, :])
        inner = ((1,), (0,))
        products = dot(high, row_high, inner) + (
            dot(high, row_rest, inner) + dot(rest, row_high, inner)
        )
        square = total * total
        lane = lax.broadcasted_iota(jnp.int32, (tokens, 128), 1)
        sums = square[:, :128] + square[:, 128:]
        stats[...] += products + jnp.where(
            lane == 0, jnp.sum(sums, axis=1, keepdims=True), 0.0
        )

    stats_ref[...] = stats[...].T[:24]


def hidden_and_stats(place, heads, first, second, own, other, resid, down, up, rows):
    tokens, cols = heads.shape
    vmem = pl.BlockSpec(memory_space=pltpu.VMEM)
    hbm = pl.BlockSpec(memory_space=pl.ANY)
    smem = pl.BlockSpec(memory_space=pltpu.SMEM)
    return pl.pallas_call(
        hidden_kernel,
        out_shape=(
            jax.ShapeDtypeStruct((tokens, cols), f32),
            jax.ShapeDtypeStruct((16, tokens), bf16),
            jax.ShapeDtypeStruct((24, tokens), f32),
        ),
        in_specs=[smem] + [hbm] * 5 + [vmem] * 4,
        out_specs=(vmem, vmem, vmem),
        scratch_shapes=[
            pltpu.VMEM((tokens, 4 * cols), bf16),
            pltpu.VMEM((4, 16, 4, 64, 256), bf16),
            pltpu.VMEM((tokens, 128), f32),
            pltpu.SemaphoreType.DMA((11,)),
        ],
        compiler_params=pltpu.CompilerParams(vmem_limit_bytes=48 * 1024 * 1024),
        cost_estimate=pl.CostEstimate(
            flops=2 * tokens * 4096 * cols, bytes_accessed=16 * 2**20, transcendentals=0
        ),
    )(place, heads, first, second, own, other, resid, down, up, rows)


def shards(
    query_embedding_cache,
    passage_embedding_cache,
    positive,
    heads,
    residual,
    output_projection_weight,
    final_norm_gain,
    adapter_down_weight,
    adapter_up_weight,
    sequence_length,
):
    tokens, cols = heads.shape
    width = adapter_down_weight.shape[1]
    mp = lax.axis_index("mp")
    core = lax.axis_index("core")
    length = sequence_length[0]
    cut = tokens // 2
    near = gather_near(heads[:cut])
    line, pairs = gather_line(
        output_projection_weight, query_embedding_cache, passage_embedding_cache, positive
    )
    own = gather(line, ("x", "y")).reshape(16, 4, 64, 512)
    packed = spread(pairs, ("x", "y"), 16)
    near, packed = lax.optimization_barrier((near, packed))
    query_grad, passage_grad = pair_grads(
        query_embedding_cache, passage_embedding_cache, packed
    )
    first = gather_far(*near)
    own, first, passage_grad = lax.optimization_barrier((own, first, passage_grad))
    count = jnp.clip((length - cut + 63) // 64, 0, cut // 64)
    rest = lax.optimization_barrier((heads[cut:], first))[0]
    second = gather_valid(rest, count)
    other = lax.ppermute(own, "core", [(0, 1), (1, 0)])
    upper = lax.dynamic_slice_in_dim(passage_grad, mp * cols, cols, 1)
    scaled = final_norm_gain[None, :] * upper

    up_wide = adapter_up_weight.astype(f32)
    scaled_up = jnp.sum(up_wide * scaled, axis=1)[None, :]
    hidden, low_bf, stats = hidden_and_stats(
        jnp.stack([mp, core]).astype(jnp.int32),
        heads,
        first,
        second,
        own,
        other,
        residual,
        adapter_down_weight,
        adapter_up_weight,
        jnp.pad(jnp.concatenate([scaled, up_wide]), ((1, 110), (0, 0))).T,
    )
    stats = jnp.concatenate(
        [
            stats[0:18],
            jnp.pad(scaled_up, ((0, 0), (0, tokens - 16))),
            jnp.zeros((5, tokens), f32),
        ]
    )
    stats = jnp.sum(spread(stats, "mp", 4).reshape(4, 24, tokens), axis=0)
    sumsq, dot_row, hidden_up = stats[0:1], stats[1:2], stats[2:18]
    scaled_up = stats[18, :16][:, None]
    inverse = lax.rsqrt(sumsq / width + norm_floor)
    factor = inverse**3 * dot_row / width
    positions = lax.broadcasted_iota(jnp.int32, (1, tokens), 1)
    mask = (positions < length).astype(f32) / length.astype(f32)
    low_grad = 2.0 * mask * (scaled_up * inverse - hidden_up * factor)
    down_term = dot(heads, low_grad.astype(bf16), ((0,), (1,)))
    low_wide = low_bf.astype(f32)
    hidden_grad = mask.reshape(tokens, 1) * (
        scaled * inverse.reshape(tokens, 1) - hidden * factor.reshape(tokens, 1)
    )
    up_term = 2.0 * dot(hidden_grad, low_wide, ((0,), (1,)), lax.Precision.HIGHEST)
    terms = jnp.concatenate([down_term, up_term], axis=1).reshape(128, 8, 32)
    terms = lax.all_to_all(terms, ("x", "zl"), 0, 0, tiled=True)
    terms = jnp.sum(terms.reshape(16, 8, 8, 32), axis=0)
    terms = jnp.sum(lax.all_to_all(terms, ("y", "core"), 0, 0, tiled=True), axis=0)
    return query_grad, passage_grad, terms[:, :16].T, terms[:, 16:].T


def solution(mesh):
    fine = Mesh(mesh.devices.reshape(SIZES), AXES)
    both = P(DP, "mp")
    placed = (
        P(DP, None),
        P(DP, None),
        P(DP),
        both,
        both,
        both,
        P("mp"),
        P(),
        P(None, "mp"),
        P(DP),
    )
    last = P(None, ("mp",) + DP)
    return jax.shard_map(
        shards,
        mesh=fine,
        in_specs=placed,
        out_specs=(P(DP, None), P(DP, None), last, last),
        check_vma=False,
    )
```

time: 2170 us -> 276 us (0.13)
  waiting for transfers between devices: 1650 us -> 87.3 us
  blocking collectives: 454 us -> 22.3 us
  starting transfers between devices: 0.2 us -> 105 us
  matrix products: 31.2 us -> 6.89 us
    unnamed x6 -> x1, waiting for transfers between devices: 1310 us -> 0.02 us
    unnamed x2 -> x0, blocking collectives: 419 us -> none
    all_gather x4 -> x1, waiting for transfers between devices: 344 us -> 0.02 us  [gather(): return lax.all_gather(rows, axes, axis=0, tiled=True)]
    all_to_all x0 -> x4, starting transfers between devices: none -> 80.5 us  [the longest x2 36.1 us: spread(): lax.all_to_all(copies, axis, 0, 0, tiled=True).reshape(-1, rows.shape[1])]
    ppermute x0 -> x5, waiting for transfers between devices: none -> 67.4 us  [the longest x1 30.2 us: gather_near(): lax.ppermute(part, 'mp', ring(1))]
    psum x2 -> x0, blocking collectives: 34.4 us -> none  [the longest x1 20.2 us: shards(): low_grad = 2.0 * lax.psum(low_part, 'mp')]
    dot_general x10 -> x5, matrix products: 31.2 us -> 6.89 us  [dot(): lax.dot_general(left, right, (dims, ((), ())), precision=precision, prefe...]
    ppermute x0 -> x5, starting transfers between devices: none -> 24.2 us  [the longest x1 8.81 us: gather_near(): lax.ppermute(part, 'mp', ring(1))]
  transfers between devices with their start and end apart: 5 -> 10, of which waited for: 3 -> 8; matrix products, arithmetic and copies ran while one was open for 1% -> 6% of each run, Pallas kernels for 0% -> 0%
where the time goes in v1:
time: 276 us; the launch traced here: 275 us
  starting transfers between devices  105 us (38%)
  waiting for transfers between devices  87.3 us (32%)
  blocking collectives  22.3 us (8%)
  between operations  17.2 us (6%)
  local copies, waits for them, and re-layouts  15.1 us (5%)
  Pallas kernels  12.1 us (4%)
  other arithmetic  9.63 us (3%)
  matrix products  6.89 us (2%)
    all_to_all x2, starting transfers between devices, spread(): lax.all_to_all(copies, axis, 0, 0, tiled=True).reshape(-1, rows.shape[1])  36.1 us
    ppermute x1, waiting for transfers between devices, gather_near(): lax.ppermute(part, 'mp', ring(1))  30.2 us
    all_to_all x1, starting transfers between devices, shards(): lax.all_to_all(terms, ('y', 'core'), 0, 0, tiled=True)  26 us
    all_to_all x1, blocking collectives, gather_line(): line = lax.all_to_all(sent, ('zl', 'core'), 0, 0, tiled=True)  22.3 us
    ppermute x1, waiting for transfers between devices, gather_near(): lax.ppermute(part, 'mp', ring(3))  21.4 us
    all_to_all x1, starting transfers between devices, shards(): terms = lax.all_to_all(terms, ('x', 'zl'), 0, 0, tiled=True)  18.4 us
    all_to_all x2, waiting for transfers between devices, spread(): lax.all_to_all(copies, axis, 0, 0, tiled=True).reshape(-1, rows.shape[1])  12.8 us
    pallas_call x1, Pallas kernels, hidden_and_stats(): pl.pallas_call(hidden_kernel, out_shape=(jax.ShapeDtypeStruct((tokens, co...  12.1 us
  transfers between devices with their start and end apart: 10, of which 8 were waited for; matrix products, arithmetic and copies ran while one was open for 6% of the time, Pallas kernels for 0%

profile of v1, /device:TPU:1, one launch (start us, length us, event | category | flops | bytes accessed | tf_op | source)
XLA Modules:
  0.0 275.3 jit_solution(2405915218262434030)
XLA Ops:
  10.9 22.3 %all_to_all.25 = bf16[8,50,512]{2,1,0:T(8,128)(2,1)S(1)} all-to-all(bf16[8,50,512]{2,1,0:T(8,128)(2,1)S(1)} %constant_dynamic-update-slice_fusion), channel_id=1, replica_groups=mesh['x'=4,'zl'=4,'y'=4,'core'=2,'mp'=4] {'zl','core'}, dimensions={0} | all-to-all | bytes 819200 | tf_op jit(solution)/shard_map/all_to_all | solution.py:53
  34.1 1.5 broadcast_in_dim.28
  35.6 4.8 %all-to-all-start.1 = ((bf16[16,8,8320]{2,1,0:T(8,128)(2,1)}), bf16[16,8,8320]{2,1,0:T(8,128)(2,1)S(1)}, u32[]{:S(2)}, u32[]{:S(2)}) async-start(bf16[16,8,8320]{2,1,0:T(8,128)(2,1)} %broadcast_in_dim.28), calls=%async_computation.1 | async-start | bytes 4259840 | tf_op jit(solution)/shard_map/all_to_all | solution.py:34
  41.5 8.8 %collective-permute-start.16 = (bf16[256,1024]{1,0:T(8,128)(2,1)}, bf16[256,1024]{1,0:T(8,128)(2,1)}, u32[]{:S(2)}, u32[]{:S(2)}) collective-permute-start(bf16[256,1024]{1,0:T(8,128)(2,1)} %get-tuple-element.53), channel_id=1, source_target_pairs={{0,1},{1,2},{2,3},{3,0},{4,5},{5,6},{6,7},{7,4},{8,9},{9,10},{10,1... | collective-permute-start | bytes 1572872 | tf_op jit(solution)/shard_map/ppermute | solution.py:87
  50.3 2.9 %collective-permute-start.17 = (bf16[256,1024]{1,0:T(8,128)(2,1)}, bf16[256,1024]{1,0:T(8,128)(2,1)}, u32[]{:S(2)}, u32[]{:S(2)}) collective-permute-start(bf16[256,1024]{1,0:T(8,128)(2,1)} %get-tuple-element.53), channel_id=1, source_target_pairs={{0,3},{1,0},{2,1},{3,2},{4,7},{5,4},{6,5},{7,6},{8,11},{9,8},{10,9... | collective-permute-start | bytes 1572872 | tf_op jit(solution)/shard_map/ppermute | solution.py:87
  54.5 30.2 %collective-permute-done.16 = bf16[256,1024]{1,0:T(8,128)(2,1)} collective-permute-done((bf16[256,1024]{1,0:T(8,128)(2,1)}, bf16[256,1024]{1,0:T(8,128)(2,1)}, u32[]{:S(2)}, u32[]{:S(2)}) %collective-permute-start.16) | collective-permute-done | bytes 524320 | tf_op jit(solution)/shard_map/ppermute | solution.py:87
  84.7 21.4 %collective-permute-done.17 = bf16[256,1024]{1,0:T(8,128)(2,1)} collective-permute-done((bf16[256,1024]{1,0:T(8,128)(2,1)}, bf16[256,1024]{1,0:T(8,128)(2,1)}, u32[]{:S(2)}, u32[]{:S(2)}) %collective-permute-start.17) | collective-permute-done | bytes 524320 | tf_op jit(solution)/shard_map/ppermute | solution.py:87
  108.3 3.9 %collective-permute-start.19 = (bf16[128,1024]{1,0:T(8,128)(2,1)S(1)}, bf16[128,1024]{1,0:T(8,128)(2,1)S(1)}, u32[]{:S(2)}, u32[]{:S(2)}) collective-permute-start(bf16[128,1024]{1,0:T(8,128)(2,1)S(1)} %slice.100), channel_id=1, source_target_pairs={{0,3},{1,0},{2,1},{3,2},{4,7},{5,4},{6,5},{7,6},{8,11},{9,8},{10,9... | collective-permute-start | bytes 786440 | tf_op jit(solution)/shard_map/ppermute | solution.py:93
  113.2 5.3 %collective-permute-start.18 = (bf16[128,1024]{1,0:T(8,128)(2,1)S(1)}, bf16[128,1024]{1,0:T(8,128)(2,1)S(1)}, u32[]{:S(2)}, u32[]{:S(2)}) collective-permute-start(bf16[128,1024]{1,0:T(8,128)(2,1)S(1)} %slice.99), channel_id=1, source_target_pairs={{0,1},{1,2},{2,3},{3,0},{4,5},{5,6},{6,7},{7,4},{8,9},{9,10},{10,1... | collective-permute-start | bytes 786440 | tf_op jit(solution)/shard_map/ppermute | solution.py:92
  120.5 8.5 %collective-permute-done.19 = bf16[128,1024]{1,0:T(8,128)(2,1)S(1)} collective-permute-done((bf16[128,1024]{1,0:T(8,128)(2,1)S(1)}, bf16[128,1024]{1,0:T(8,128)(2,1)S(1)}, u32[]{:S(2)}, u32[]{:S(2)}) %collective-permute-start.19) | collective-permute-done | bytes 262176 | tf_op jit(solution)/shard_map/ppermute | solution.py:93
  129.0 5.0 %collective-permute-done.18 = bf16[128,1024]{1,0:T(8,128)(2,1)S(1)} collective-permute-done((bf16[128,1024]{1,0:T(8,128)(2,1)S(1)}, bf16[128,1024]{1,0:T(8,128)(2,1)S(1)}, u32[]{:S(2)}, u32[]{:S(2)}) %collective-permute-start.18) | collective-permute-done | bytes 262176 | tf_op jit(solution)/shard_map/ppermute | solution.py:92
  135.4 3.4 %collective-permute-start.20 = (bf16[16,4,64,512]{3,2,1,0:T(8,128)(2,1)}, bf16[16,4,64,512]{3,2,1,0:T(8,128)(2,1)}, u32[]{:S(2)}, u32[]{:S(2)}) collective-permute-start(bf16[16,4,64,512]{3,2,1,0:T(8,128)(2,1)} %bitcast.116), channel_id=1, source_target_pairs={{0,4},{4,0},{1,5},{5,1},{2,6},{6,2},{3,7},{7,3},{8,12},{12,8},{9,1... | collective-permute-start | bytes 12582920 | tf_op jit(solution)/shard_map/ppermute | solution.py:244
  140.8 1.4 conditional.1
  140.8 1.4 broadcast.272
  143.5 2.4 collective-permute-done.20.other_ref
  147.1 12.1 %shard_map.129 = (f32[512,1024]{1,0:T(8,128)}, bf16[16,512]{1,0:T(8,128)(2,1)S(1)}, f32[24,512]{1,0:T(8,128)S(1)}) custom-call(s32[2]{0:T(128)S(1)} %pad_add_fusion.place_ref, bf16[512,1024]{1,0:T(8,128)(2,1)S(1)} %copy-done, bf16[3,256,1024]{2,1,0:T(8,128)(2,1)S(1)} %pad_maximum_fusion.1.first_ref, bf16[3,256,1024]{2,1,0:T(8,128)(2,1)} %get-tuple-element.68.second_ref, ...), custom_call_target="tpu_custom_call" | custom-call | flops 4294967296 | bytes 16777216 | tf_op jit(solution)/shard_map/pallas_call | solution.py:189
  160.0 31.3 %all-to-all-start.2 = ((f32[4,24,512]{2,1,0:T(8,128)}), f32[4,24,512]{2,1,0:T(8,128)S(1)}, u32[]{:S(2)}, u32[]{:S(2)}) async-start(f32[4,24,512]{2,1,0:T(8,128)} %broadcast_in_dim.57), calls=%async_computation.2 | async-start | bytes 393216 | tf_op jit(solution)/shard_map/all_to_all | solution.py:34
  191.4 12.8 %all-to-all-done.2 = f32[4,24,512]{2,1,0:T(8,128)S(1)} async-done(((f32[4,24,512]{2,1,0:T(8,128)}), f32[4,24,512]{2,1,0:T(8,128)S(1)}, u32[]{:S(2)}, u32[]{:S(2)}) %all-to-all-start.2) | async-done | bytes 196640 | tf_op jit(solution)/shard_map/all_to_all | solution.py:34
  204.5 2.7 fusion.24
  208.3 18.4 %all-to-all-start.3 = ((f32[16,1,2048]{2,1,0:T(1,128)}), f32[16,1,2048]{2,1,0:T(1,128)S(1)}, u32[]{:S(2)}, u32[]{:S(2)}) async-start(f32[16,1,2048]{2,1,0:T(1,128)} %reshape.288), calls=%async_computation.3 | async-start | bytes 262144 | tf_op jit(solution)/shard_map/all_to_all | solution.py:284
  228.1 2.2 multiply_reduce_fusion.3
  230.3 3.7 %all-to-all-done.3 = f32[16,1,2048]{2,1,0:T(1,128)S(1)} async-done(((f32[16,1,2048]{2,1,0:T(1,128)}), f32[16,1,2048]{2,1,0:T(1,128)S(1)}, u32[]{:S(2)}, u32[]{:S(2)}) %all-to-all-start.3) | async-done | bytes 131104 | tf_op jit(solution)/shard_map/all_to_all | solution.py:284
  236.4 26.0 %all-to-all-start.4 = ((f32[8,1,256]{2,1,0:T(1,128)}), f32[8,1,256]{2,1,0:T(1,128)S(1)}, u32[]{:S(2)}, u32[]{:S(2)}) async-start(f32[8,1,256]{2,1,0:T(1,128)} %reshape.290), calls=%async_computation.4 | async-start | bytes 16384 | tf_op jit(solution)/shard_map/all_to_all | solution.py:286
  263.7 3.3 %all-to-all-done.4 = f32[8,1,256]{2,1,0:T(1,128)S(1)} async-done(((f32[8,1,256]{2,1,0:T(1,128)}), f32[8,1,256]{2,1,0:T(1,128)S(1)}, u32[]{:S(2)}, u32[]{:S(2)}) %all-to-all-start.4) | async-done | bytes 8224 | tf_op jit(solution)/shard_map/all_to_all | solution.py:286
  (91 shorter events, 24.0 us)
Async XLA Ops:
  7.2 128.3 %all-gather.2.cloned.1.call-start = ((), (), s32[]{:S(2)}) async-start(), calls=%async_computation.5 | async-start | bytes 4456448 | tf_op jit(solution)/shard_map/all_gather | solution.py:29
  35.6 4.8 %copy-start = (bf16[512,1024]{1,0:T(8,128)(2,1)S(1)}, bf16[512,1024]{1,0:T(8,128)(2,1)}, u32[]{:S(2)}) copy-start(bf16[512,1024]{1,0:T(8,128)(2,1)} %heads_ref.1) | copy-start | bytes 3145732
  35.6 70.5 %all-to-all-start.1 = ((bf16[16,8,8320]{2,1,0:T(8,128)(2,1)}), bf16[16,8,8320]{2,1,0:T(8,128)(2,1)S(1)}, u32[]{:S(2)}, u32[]{:S(2)}) async-start(bf16[16,8,8320]{2,1,0:T(8,128)(2,1)} %broadcast_in_dim.28), calls=%async_computation.1 | async-start | bytes 4259840 | tf_op jit(solution)/shard_map/all_to_all | solution.py:34
  40.4 12.8 %copy-start.6 = (bf16[1,4096]{1,0:T(2,128)(2,1)S(1)}, bf16[1,4096]{1,0:T(2,128)(2,1)}, u32[]{:S(2)}) copy-start(bf16[1,4096]{1,0:T(2,128)(2,1)} %param.16) | copy-start | bytes 24580
  41.5 43.2 %collective-permute-start.16 = (bf16[256,1024]{1,0:T(8,128)(2,1)}, bf16[256,1024]{1,0:T(8,128)(2,1)}, u32[]{:S(2)}, u32[]{:S(2)}) collective-permute-start(bf16[256,1024]{1,0:T(8,128)(2,1)} %get-tuple-element.53), channel_id=1, source_target_pairs={{0,1},{1,2},{2,3},{3,0},{4,5},{5,6},{6,7},{7,4},{8,9},{9,10},{10,1... | collective-permute-start | bytes 1572872 | tf_op jit(solution)/shard_map/ppermute | solution.py:87
  50.3 55.8 %collective-permute-start.17 = (bf16[256,1024]{1,0:T(8,128)(2,1)}, bf16[256,1024]{1,0:T(8,128)(2,1)}, u32[]{:S(2)}, u32[]{:S(2)}) collective-permute-start(bf16[256,1024]{1,0:T(8,128)(2,1)} %get-tuple-element.53), channel_id=1, source_target_pairs={{0,3},{1,0},{2,1},{3,2},{4,7},{5,4},{6,5},{7,6},{8,11},{9,8},{10,9... | collective-permute-start | bytes 1572872 | tf_op jit(solution)/shard_map/ppermute | solution.py:87
  106.1 12.7 %copy-start.4 = (bf16[16,8,8320]{2,1,0:T(8,128)(2,1)}, bf16[16,8,8320]{2,1,0:T(8,128)(2,1)S(1)}, u32[]{:S(2)}) copy-start(bf16[16,8,8320]{2,1,0:T(8,128)(2,1)S(1)} %all-to-all-done.1) | copy-start | bytes 6389764
  108.3 20.7 %collective-permute-start.19 = (bf16[128,1024]{1,0:T(8,128)(2,1)S(1)}, bf16[128,1024]{1,0:T(8,128)(2,1)S(1)}, u32[]{:S(2)}, u32[]{:S(2)}) collective-permute-start(bf16[128,1024]{1,0:T(8,128)(2,1)S(1)} %slice.100), channel_id=1, source_target_pairs={{0,3},{1,0},{2,1},{3,2},{4,7},{5,4},{6,5},{7,6},{8,11},{9,8},{10,9... | collective-permute-start | bytes 786440 | tf_op jit(solution)/shard_map/ppermute | solution.py:93
  113.2 20.8 %collective-permute-start.18 = (bf16[128,1024]{1,0:T(8,128)(2,1)S(1)}, bf16[128,1024]{1,0:T(8,128)(2,1)S(1)}, u32[]{:S(2)}, u32[]{:S(2)}) collective-permute-start(bf16[128,1024]{1,0:T(8,128)(2,1)S(1)} %slice.99), channel_id=1, source_target_pairs={{0,1},{1,2},{2,3},{3,0},{4,5},{5,6},{6,7},{7,4},{8,9},{9,10},{10,1... | collective-permute-start | bytes 786440 | tf_op jit(solution)/shard_map/ppermute | solution.py:92
  120.5 19.2 %copy-start.8 = (f32[1,4096]{1,0:T(1,128)}, f32[1,4096]{1,0:T(1,128)S(1)}, u32[]{:S(2)}) copy-start(f32[1,4096]{1,0:T(1,128)S(1)} %subtract_multiply_fusion) | copy-start | bytes 49156
  120.5 19.0 %copy-start.1 = (bf16[16,1024]{1,0:T(8,128)(2,1)S(1)}, bf16[16,1024]{1,0:T(8,128)(2,1)}, u32[]{:S(2)}) copy-start(bf16[16,1024]{1,0:T(8,128)(2,1)} %up_ref.1) | copy-start | bytes 98308
  120.5 19.2 %copy-start.9 = (f32[1024]{0:T(1024)S(1)}, f32[1024]{0:T(1024)}, u32[]{:S(2)}) copy-start(f32[1024]{0:T(1024)} %param.21) | copy-start | bytes 12292
  120.5 19.2 %copy-start.5 = (bf16[256,1024]{1,0:T(8,128)(2,1)S(1)}, bf16[256,1024]{1,0:T(8,128)(2,1)}, u32[]{:S(2)}) copy-start(bf16[256,1024]{1,0:T(8,128)(2,1)} %get-tuple-element.29) | copy-start | bytes 1572868
  135.4 10.5 %collective-permute-start.20 = (bf16[16,4,64,512]{3,2,1,0:T(8,128)(2,1)}, bf16[16,4,64,512]{3,2,1,0:T(8,128)(2,1)}, u32[]{:S(2)}, u32[]{:S(2)}) collective-permute-start(bf16[16,4,64,512]{3,2,1,0:T(8,128)(2,1)} %bitcast.116), channel_id=1, source_target_pairs={{0,4},{4,0},{1,5},{5,1},{2,6},{6,2},{3,7},{7,3},{8,12},{12,8},{9,1... | collective-permute-start | bytes 12582920 | tf_op jit(solution)/shard_map/ppermute | solution.py:244
  140.8 5.1 %copy-start.3 = (bf16[16,4096]{1,0:T(8,128)(2,1)S(1)}, bf16[16,4096]{1,0:T(8,128)(2,1)}, u32[]{:S(2)}) copy-start(bf16[16,4096]{1,0:T(8,128)(2,1)} %down_ref.1) | copy-start | bytes 393220
  145.9 1.2 copy-start.2
  160.0 44.1 %all-to-all-start.2 = ((f32[4,24,512]{2,1,0:T(8,128)}), f32[4,24,512]{2,1,0:T(8,128)S(1)}, u32[]{:S(2)}, u32[]{:S(2)}) async-start(f32[4,24,512]{2,1,0:T(8,128)} %broadcast_in_dim.57), calls=%async_computation.2 | async-start | bytes 393216 | tf_op jit(solution)/shard_map/all_to_all | solution.py:34
  204.5 22.3 %copy-start.7 = (bf16[1,4096]{1,0:T(2,128)(2,1)S(1)}, bf16[1,4096]{1,0:T(2,128)(2,1)}, u32[]{:S(2)}) copy-start(bf16[1,4096]{1,0:T(2,128)(2,1)} %param.15) | copy-start | bytes 24580
  208.3 25.7 %all-to-all-start.3 = ((f32[16,1,2048]{2,1,0:T(1,128)}), f32[16,1,2048]{2,1,0:T(1,128)S(1)}, u32[]{:S(2)}, u32[]{:S(2)}) async-start(f32[16,1,2048]{2,1,0:T(1,128)} %reshape.288), calls=%async_computation.3 | async-start | bytes 262144 | tf_op jit(solution)/shard_map/all_to_all | solution.py:284
  236.4 30.6 %all-to-all-start.4 = ((f32[8,1,256]{2,1,0:T(1,128)}), f32[8,1,256]{2,1,0:T(1,128)S(1)}, u32[]{:S(2)}, u32[]{:S(2)}) async-start(f32[8,1,256]{2,1,0:T(1,128)} %reshape.290), calls=%async_computation.4 | async-start | bytes 16384 | tf_op jit(solution)/shard_map/all_to_all | solution.py:286
Sparse Core Ops, SparseCore 0:
  34.1 77.6 all-gather.1

commit v2 on v1

--- a/solution.py
+++ b/solution.py
@@ -94,19 +94,18 @@
     return jnp.stack([before, after, jnp.concatenate([left, right])])
 
 
-def gather_valid(part, count):
+def gather_valid(part, count, step):
     tokens, cols = part.shape
 
     def prefix(size):
         def branch(rows):
-            if size == 0:
-                return jnp.zeros((3, tokens, cols), rows.dtype)
             blocks = gather_far(*gather_near(rows[:size]))
             return jnp.pad(blocks, ((0, 0), (0, tokens - size), (0, 0)))
 
         return branch
 
-    return lax.switch(count, [prefix(size) for size in range(0, tokens + 1, 64)], part)
+    sizes = range(step, tokens + 1, step)
+    return lax.switch(count - 1, [prefix(size) for size in sizes], part)
 
 
 def split(values):
@@ -115,21 +114,16 @@
 
 
 def hidden_kernel(
-    place_ref, heads_ref, first_ref, second_ref, own_ref, other_ref, resid_ref, down_ref, up_ref,
+    place_ref, heads_ref, blocks_ref, own_ref, other_ref, resid_ref, down_ref, up_ref,
     rows_ref, hidden_ref, low_ref, stats_ref, heads, weights, stats, sems
 ):
     mp, core = place_ref[0], place_ref[1]
     tokens, cols = heads_ref.shape
-    cut = first_ref.shape[1]
     copies = []
     for i in range(4):
         at = pl.ds(pl.multiple_of(lax.rem(mp + (0, 3, 1, 2)[i], 4) * cols, cols), cols)
-        if i == 0:
-            copies.append(pltpu.make_async_copy(heads_ref, heads.at[:, at], sems.at[4]))
-            continue
-        for k, ref in enumerate((first_ref, second_ref)):
-            part = heads.at[pl.ds(k * cut, cut), at]
-            copies.append(pltpu.make_async_copy(ref.at[i - 1], part, sems.at[3 + 2 * i + k]))
+        source = blocks_ref.at[i - 1] if i else heads_ref
+        copies.append(pltpu.make_async_copy(source, heads.at[:, at], sems.at[4 + i]))
     early = len(copies)
     for i in range(4):
         ref = own_ref if i < 2 else other_ref
@@ -181,7 +175,7 @@
     stats_ref[...] = stats[...].T[:24]
 
 
-def hidden_and_stats(place, heads, first, second, own, other, resid, down, up, rows):
+def hidden_and_stats(place, heads, blocks, own, other, resid, down, up, rows):
     tokens, cols = heads.shape
     vmem = pl.BlockSpec(memory_space=pltpu.VMEM)
     hbm = pl.BlockSpec(memory_space=pl.ANY)
@@ -193,19 +187,19 @@
             jax.ShapeDtypeStruct((16, tokens), bf16),
             jax.ShapeDtypeStruct((24, tokens), f32),
         ),
-        in_specs=[smem] + [hbm] * 5 + [vmem] * 4,
+        in_specs=[smem] + [hbm] * 4 + [vmem] * 4,
         out_specs=(vmem, vmem, vmem),
         scratch_shapes=[
             pltpu.VMEM((tokens, 4 * cols), bf16),
             pltpu.VMEM((4, 16, 4, 64, 256), bf16),
             pltpu.VMEM((tokens, 128), f32),
-            pltpu.SemaphoreType.DMA((11,)),
+            pltpu.SemaphoreType.DMA((8,)),
         ],
         compiler_params=pltpu.CompilerParams(vmem_limit_bytes=48 * 1024 * 1024),
         cost_estimate=pl.CostEstimate(
             flops=2 * tokens * 4096 * cols, bytes_accessed=16 * 2**20, transcendentals=0
         ),
-    )(place, heads, first, second, own, other, resid, down, up, rows)
+    )(place, heads, blocks, own, other, resid, down, up, rows)
 
 
 def shards(
@@ -225,23 +219,20 @@
     mp = lax.axis_index("mp")
     core = lax.axis_index("core")
     length = sequence_length[0]
-    cut = tokens // 2
-    near = gather_near(heads[:cut])
+    step = 32
     line, pairs = gather_line(
         output_projection_weight, query_embedding_cache, passage_embedding_cache, positive
     )
+    rows, line = lax.optimization_barrier((heads, line))
     own = gather(line, ("x", "y")).reshape(16, 4, 64, 512)
+    count = (length + step - 1) // step
+    blocks = gather_valid(rows, count, step)
+    own, blocks, pairs = lax.optimization_barrier((own, blocks, pairs))
     packed = spread(pairs, ("x", "y"), 16)
-    near, packed = lax.optimization_barrier((near, packed))
+    other = lax.ppermute(own, "core", [(0, 1), (1, 0)])
     query_grad, passage_grad = pair_grads(
         query_embedding_cache, passage_embedding_cache, packed
     )
-    first = gather_far(*near)
-    own, first, passage_grad = lax.optimization_barrier((own, first, passage_grad))
-    count = jnp.clip((length - cut + 63) // 64, 0, cut // 64)
-    rest = lax.optimization_barrier((heads[cut:], first))[0]
-    second = gather_valid(rest, count)
-    other = lax.ppermute(own, "core", [(0, 1), (1, 0)])
     upper = lax.dynamic_slice_in_dim(passage_grad, mp * cols, cols, 1)
     scaled = final_norm_gain[None, :] * upper
 
@@ -250,8 +241,7 @@
     hidden, low_bf, stats = hidden_and_stats(
         jnp.stack([mp, core]).astype(jnp.int32),
         heads,
-        first,
-        second,
+        blocks,
         own,
         other,
         residual,

time: 276 us -> 274 us (level)
  waiting for transfers between devices: 87.3 us -> 115 us
  starting transfers between devices: 105 us -> 80 us
  local copies, waits for them, and re-layouts: 15.1 us -> 7.7 us
  other arithmetic: 9.63 us -> 12.4 us
    ppermute x1, waiting for transfers between devices: 21.4 us -> 57 us  [gather_near(): lax.ppermute(part, 'mp', ring(3))]
    ppermute x1, waiting for transfers between devices: 30.2 us -> 0.01 us  [gather_near(): lax.ppermute(part, 'mp', ring(1))]
    all_to_all x2, waiting for transfers between devices: 12.8 us -> 36.4 us  [spread(): lax.all_to_all(copies, axis, 0, 0, tiled=True).reshape(-1, rows.shape[1])]
    all_to_all x1, starting transfers between devices: 26 us -> 8.57 us  [shards(): lax.all_to_all(terms, ('y', 'core'), 0, 0, tiled=True)]
    ppermute x1, starting transfers between devices: 8.81 us -> 1.92 us  [gather_near(): lax.ppermute(part, 'mp', ring(1))]
    all_to_all x1, starting transfers between devices: 18.4 us -> 12.5 us  [shards(): terms = lax.all_to_all(terms, ('x', 'zl'), 0, 0, tiled=True)]
    ppermute x1, starting transfers between devices: 2.86 us -> 7.69 us  [gather_near(): lax.ppermute(part, 'mp', ring(3))]
  transfers between devices with their start and end apart: 10 -> 10, of which waited for: 8 -> 7; matrix products, arithmetic and copies ran while one was open for 6% -> 6% of each run, Pallas kernels for 0% -> 0%
where the time goes in v2:
time: 274 us; the launch traced here: 276 us
  waiting for transfers between devices  115 us (42%)
  starting transfers between devices  80 us (29%)
  blocking collectives  22.3 us (8%)
  between operations  17.3 us (6%)
  other arithmetic  12.4 us (5%)
  Pallas kernels  11.8 us (4%)
  matrix products  9.33 us (3%)
  local copies, waits for them, and re-layouts  7.7 us (3%)
    ppermute x1, waiting for transfers between devices, gather_near(): lax.ppermute(part, 'mp', ring(3))  57 us
    all_to_all x2, starting transfers between devices, spread(): lax.all_to_all(copies, axis, 0, 0, tiled=True).reshape(-1, rows.shape[1])  38.2 us
    all_to_all x2, waiting for transfers between devices, spread(): lax.all_to_all(copies, axis, 0, 0, tiled=True).reshape(-1, rows.shape[1])  36.4 us
    all_to_all x1, blocking collectives, gather_line(): line = lax.all_to_all(sent, ('zl', 'core'), 0, 0, tiled=True)  22.3 us
    all_to_all x1, starting transfers between devices, shards(): terms = lax.all_to_all(terms, ('x', 'zl'), 0, 0, tiled=True)  12.5 us
    pallas_call x1, Pallas kernels, hidden_and_stats(): pl.pallas_call(hidden_kernel, out_shape=(jax.ShapeDtypeStruct((tokens, co...  11.8 us
    dot_general x5, matrix products, dot(): lax.dot_general(left, right, (dims, ((), ())), precision=precision, prefe...  9.33 us
    all_to_all x1, starting transfers between devices, shards(): lax.all_to_all(terms, ('y', 'core'), 0, 0, tiled=True)  8.57 us
  transfers between devices with their start and end apart: 10, of which 7 were waited for; matrix products, arithmetic and copies ran while one was open for 6% of the time, Pallas kernels for 0%

profile of v2, /device:TPU:1, one launch (start us, length us, event | category | flops | bytes accessed | tf_op | source)
XLA Modules:
  0.0 275.5 jit_solution(15032875407021447349)
XLA Ops:
  11.0 22.3 %all_to_all.25 = bf16[8,50,512]{2,1,0:T(8,128)(2,1)S(1)} all-to-all(bf16[8,50,512]{2,1,0:T(8,128)(2,1)S(1)} %constant_dynamic-update-slice_fusion), channel_id=1, replica_groups=mesh['x'=4,'zl'=4,'y'=4,'core'=2,'mp'=4] {'zl','core'}, dimensions={0} | all-to-all | bytes 819200 | tf_op jit(solution)/shard_map/all_to_all | solution.py:53
  34.9 92.0 %conditional.1 = (bf16[3,512,1024]{2,1,0:T(8,128)(2,1)}) conditional(s32[]{:T(128)} %clamp.3, bf16[512,1024]{1,0:T(8,128)(2,1)S(1)} %copy-done.3, bf16[512,1024]{1,0:T(8,128)(2,1)S(1)} %copy-done.3, bf16[512,1024]{1,0:T(8,128)(2,1)S(1)} %copy-done.3, bf16[512,1024]{1,0:T(8,128)(2,1)S(1)} %copy-done.3, ...), branch_computations={%region_0.1_spmd, %region_1.2_spmd, %region_2.3_spmd, %region_3.4_... | conditional | flops 17694720 | bytes 23789736 | solution.py:108
  35.0 7.7 %collective-permute-start.13 = (bf16[128,1024]{1,0:T(8,128)(2,1)S(1)}, bf16[128,1024]{1,0:T(8,128)(2,1)S(1)}, u32[]{:S(2)}, u32[]{:S(2)}) collective-permute-start(bf16[128,1024]{1,0:T(8,128)(2,1)S(1)} %slice.133), channel_id=1, source_target_pairs={{0,3},{1,0},{2,1},{3,2},{4,7},{5,4},{6,5},{7,6},{8,11},{9,8},{10,9... | collective-permute-start | bytes 786440 | tf_op jit(solution)/shard_map/cond/branch_3_fun/ppermute | solution.py:87
  42.6 1.9 collective-permute-start.12
  44.6 57.0 %collective-permute-done.13 = bf16[128,1024]{1,0:T(8,128)(2,1)S(1)} collective-permute-done((bf16[128,1024]{1,0:T(8,128)(2,1)S(1)}, bf16[128,1024]{1,0:T(8,128)(2,1)S(1)}, u32[]{:S(2)}, u32[]{:S(2)}) %collective-permute-start.13) | collective-permute-done | bytes 262176 | tf_op jit(solution)/shard_map/cond/branch_3_fun/ppermute | solution.py:87
  101.5 6.3 %collective-permute-start.15 = (bf16[64,1024]{1,0:T(8,128)(2,1)S(1)}, bf16[64,1024]{1,0:T(8,128)(2,1)S(1)}, u32[]{:S(2)}, u32[]{:S(2)}) collective-permute-start(bf16[64,1024]{1,0:T(8,128)(2,1)S(1)} %slice.208), channel_id=1, source_target_pairs={{0,3},{1,0},{2,1},{3,2},{4,7},{5,4},{6,5},{7,6},{8,11},{9,8},{10,9... | collective-permute-start | bytes 393224 | tf_op jit(solution)/shard_map/cond/branch_3_fun/ppermute | solution.py:93
  107.9 2.9 %collective-permute-start.14 = (bf16[64,1024]{1,0:T(8,128)(2,1)S(1)}, bf16[64,1024]{1,0:T(8,128)(2,1)S(1)}, u32[]{:S(2)}, u32[]{:S(2)}) collective-permute-start(bf16[64,1024]{1,0:T(8,128)(2,1)S(1)} %slice.207), channel_id=1, source_target_pairs={{0,1},{1,2},{2,3},{3,0},{4,5},{5,6},{6,7},{7,4},{8,9},{9,10},{10,1... | collective-permute-start | bytes 393224 | tf_op jit(solution)/shard_map/cond/branch_3_fun/ppermute | solution.py:92
  110.8 7.3 %collective-permute-done.15 = bf16[64,1024]{1,0:T(8,128)(2,1)S(1)} collective-permute-done((bf16[64,1024]{1,0:T(8,128)(2,1)S(1)}, bf16[64,1024]{1,0:T(8,128)(2,1)S(1)}, u32[]{:S(2)}, u32[]{:S(2)}) %collective-permute-start.15) | collective-permute-done | bytes 131104 | tf_op jit(solution)/shard_map/cond/branch_3_fun/ppermute | solution.py:93
  118.1 6.9 %collective-permute-done.14 = bf16[64,1024]{1,0:T(8,128)(2,1)S(1)} collective-permute-done((bf16[64,1024]{1,0:T(8,128)(2,1)S(1)}, bf16[64,1024]{1,0:T(8,128)(2,1)S(1)}, u32[]{:S(2)}, u32[]{:S(2)}) %collective-permute-start.14) | collective-permute-done | bytes 131104 | tf_op jit(solution)/shard_map/cond/branch_3_fun/ppermute | solution.py:92
  125.1 1.8 fusion.19
  128.4 34.8 %all-to-all-start.1 = ((bf16[16,8,8320]{2,1,0:T(8,128)(2,1)}), bf16[16,8,8320]{2,1,0:T(8,128)(2,1)}, u32[]{:S(2)}, u32[]{:S(2)}) async-start(bf16[16,8,8320]{2,1,0:T(8,128)(2,1)} %broadcast_in_dim.28), calls=%async_computation.1 | async-start | bytes 4259840 | tf_op jit(solution)/shard_map/all_to_all | solution.py:34
  163.3 1.9 collective-permute-start.64
  166.8 23.7 %all-to-all-done.1 = bf16[16,8,8320]{2,1,0:T(8,128)(2,1)} async-done(((bf16[16,8,8320]{2,1,0:T(8,128)(2,1)}), bf16[16,8,8320]{2,1,0:T(8,128)(2,1)}, u32[]{:S(2)}, u32[]{:S(2)}) %all-to-all-start.1) | async-done | bytes 2129952 | tf_op jit(solution)/shard_map/all_to_all | solution.py:34
  190.5 2.0 fusion.75
  192.6 2.3 exponential_reduce_fusion
  195.9 2.2 multiply_reduce_fusion.1
  199.5 11.8 %shard_map.129 = (f32[512,1024]{1,0:T(8,128)S(1)}, bf16[16,512]{1,0:T(8,128)(2,1)S(1)}, f32[24,512]{1,0:T(8,128)S(1)}) custom-call(s32[2]{0:T(128)S(1)} %pad_add_fusion.place_ref, bf16[512,1024]{1,0:T(8,128)(2,1)} %heads_ref.1, bf16[3,512,1024]{2,1,0:T(8,128)(2,1)} %get-tuple-element.85.blocks_ref, bf16[16,4,64,512]{3,2,1,0:T(8,128)(2,1)} %bitcast.180, ...), custom_call_target="tpu_custom_call" | custom-call | flops 4294967296 | bytes 16777216 | tf_op jit(solution)/shard_map/pallas_call | solution.py:183
  212.0 3.4 %all-to-all-start.2 = ((f32[4,24,512]{2,1,0:T(8,128)}), f32[4,24,512]{2,1,0:T(8,128)S(1)}, u32[]{:S(2)}, u32[]{:S(2)}) async-start(f32[4,24,512]{2,1,0:T(8,128)} %broadcast_in_dim.57), calls=%async_computation.2 | async-start | bytes 393216 | tf_op jit(solution)/shard_map/all_to_all | solution.py:34
  215.5 12.6 %all-to-all-done.2 = f32[4,24,512]{2,1,0:T(8,128)S(1)} async-done(((f32[4,24,512]{2,1,0:T(8,128)}), f32[4,24,512]{2,1,0:T(8,128)S(1)}, u32[]{:S(2)}, u32[]{:S(2)}) %all-to-all-start.2) | async-done | bytes 196640 | tf_op jit(solution)/shard_map/all_to_all | solution.py:34
  231.9 12.5 %all-to-all-start.3 = ((f32[16,1,2048]{2,1,0:T(1,128)}), f32[16,1,2048]{2,1,0:T(1,128)S(1)}, u32[]{:S(2)}, u32[]{:S(2)}) async-start(f32[16,1,2048]{2,1,0:T(1,128)} %reshape.288), calls=%async_computation.3 | async-start | bytes 262144 | tf_op jit(solution)/shard_map/all_to_all | solution.py:274
  245.8 2.2 multiply_reduce_fusion.3
  248.0 3.7 %all-to-all-done.3 = f32[16,1,2048]{2,1,0:T(1,128)S(1)} async-done(((f32[16,1,2048]{2,1,0:T(1,128)}), f32[16,1,2048]{2,1,0:T(1,128)S(1)}, u32[]{:S(2)}, u32[]{:S(2)}) %all-to-all-start.3) | async-done | bytes 131104 | tf_op jit(solution)/shard_map/all_to_all | solution.py:274
  254.1 8.6 %all-to-all-start.4 = ((f32[8,1,256]{2,1,0:T(1,128)}), f32[8,1,256]{2,1,0:T(1,128)S(1)}, u32[]{:S(2)}, u32[]{:S(2)}) async-start(f32[8,1,256]{2,1,0:T(1,128)} %reshape.290), calls=%async_computation.4 | async-start | bytes 16384 | tf_op jit(solution)/shard_map/all_to_all | solution.py:276
  263.9 3.4 %all-to-all-done.4 = f32[8,1,256]{2,1,0:T(1,128)S(1)} async-done(((f32[8,1,256]{2,1,0:T(1,128)}), f32[8,1,256]{2,1,0:T(1,128)S(1)}, u32[]{:S(2)}, u32[]{:S(2)}) %all-to-all-start.4) | async-done | bytes 8224 | tf_op jit(solution)/shard_map/all_to_all | solution.py:276
  (86 shorter events, 18.9 us)
Async XLA Ops:
  7.2 27.6 %copy-start.3 = (bf16[512,1024]{1,0:T(8,128)(2,1)S(1)}, bf16[512,1024]{1,0:T(8,128)(2,1)}, u32[]{:S(2)}) copy-start(bf16[512,1024]{1,0:T(8,128)(2,1)} %heads_ref.1) | copy-start | bytes 3145732
  7.2 119.7 %all-gather.2.cloned.1.call-start = ((), (), s32[]{:S(2)}) async-start(), calls=%async_computation.5 | async-start | bytes 4456448 | tf_op jit(solution)/shard_map/all_gather | solution.py:29
  35.0 66.6 %collective-permute-start.13 = (bf16[128,1024]{1,0:T(8,128)(2,1)S(1)}, bf16[128,1024]{1,0:T(8,128)(2,1)S(1)}, u32[]{:S(2)}, u32[]{:S(2)}) collective-permute-start(bf16[128,1024]{1,0:T(8,128)(2,1)S(1)} %slice.133), channel_id=1, source_target_pairs={{0,3},{1,0},{2,1},{3,2},{4,7},{5,4},{6,5},{7,6},{8,11},{9,8},{10,9... | collective-permute-start | bytes 786440 | tf_op jit(solution)/shard_map/cond/branch_3_fun/ppermute | solution.py:87
  42.6 65.2 %collective-permute-start.12 = (bf16[128,1024]{1,0:T(8,128)(2,1)S(1)}, bf16[128,1024]{1,0:T(8,128)(2,1)S(1)}, u32[]{:S(2)}, u32[]{:S(2)}) collective-permute-start(bf16[128,1024]{1,0:T(8,128)(2,1)S(1)} %slice.133), channel_id=1, source_target_pairs={{0,1},{1,2},{2,3},{3,0},{4,5},{5,6},{6,7},{7,4},{8,9},{9,10},{10,1... | collective-permute-start | bytes 786440 | tf_op jit(solution)/shard_map/cond/branch_3_fun/ppermute | solution.py:87
  101.5 16.6 %collective-permute-start.15 = (bf16[64,1024]{1,0:T(8,128)(2,1)S(1)}, bf16[64,1024]{1,0:T(8,128)(2,1)S(1)}, u32[]{:S(2)}, u32[]{:S(2)}) collective-permute-start(bf16[64,1024]{1,0:T(8,128)(2,1)S(1)} %slice.208), channel_id=1, source_target_pairs={{0,3},{1,0},{2,1},{3,2},{4,7},{5,4},{6,5},{7,6},{8,11},{9,8},{10,9... | collective-permute-start | bytes 393224 | tf_op jit(solution)/shard_map/cond/branch_3_fun/ppermute | solution.py:93
  107.9 17.1 %collective-permute-start.14 = (bf16[64,1024]{1,0:T(8,128)(2,1)S(1)}, bf16[64,1024]{1,0:T(8,128)(2,1)S(1)}, u32[]{:S(2)}, u32[]{:S(2)}) collective-permute-start(bf16[64,1024]{1,0:T(8,128)(2,1)S(1)} %slice.207), channel_id=1, source_target_pairs={{0,1},{1,2},{2,3},{3,0},{4,5},{5,6},{6,7},{7,4},{8,9},{9,10},{10,1... | collective-permute-start | bytes 393224 | tf_op jit(solution)/shard_map/cond/branch_3_fun/ppermute | solution.py:92
  126.9 38.3 %copy-start.4 = (bf16[1,4096]{1,0:T(2,128)(2,1)S(1)}, bf16[1,4096]{1,0:T(2,128)(2,1)}, u32[]{:S(2)}) copy-start(bf16[1,4096]{1,0:T(2,128)(2,1)} %param.27) | copy-start | bytes 24580
  126.9 39.6 %copy-start = (bf16[16,1024]{1,0:T(8,128)(2,1)S(1)}, bf16[16,1024]{1,0:T(8,128)(2,1)}, u32[]{:S(2)}) copy-start(bf16[16,1024]{1,0:T(8,128)(2,1)} %up_ref.1) | copy-start | bytes 98308
  128.4 62.1 %all-to-all-start.1 = ((bf16[16,8,8320]{2,1,0:T(8,128)(2,1)}), bf16[16,8,8320]{2,1,0:T(8,128)(2,1)}, u32[]{:S(2)}, u32[]{:S(2)}) async-start(bf16[16,8,8320]{2,1,0:T(8,128)(2,1)} %broadcast_in_dim.28), calls=%async_computation.1 | async-start | bytes 4259840 | tf_op jit(solution)/shard_map/all_to_all | solution.py:34
  163.3 36.2 %collective-permute-start.64 = (bf16[16,4,64,512]{3,2,1,0:T(8,128)(2,1)}, bf16[16,4,64,512]{3,2,1,0:T(8,128)(2,1)}, u32[]{:S(2)}, u32[]{:S(2)}) collective-permute-start(bf16[16,4,64,512]{3,2,1,0:T(8,128)(2,1)} %bitcast.179), channel_id=1, source_target_pairs={{0,4},{4,0},{1,5},{5,1},{2,6},{6,2},{3,7},{7,3},{8,12},{12,8},{9,1... | collective-permute-start | bytes 12582920 | tf_op jit(solution)/shard_map/ppermute | solution.py:232
  192.5 6.3 %copy-start.7 = (f32[1024]{0:T(1024)S(1)}, f32[1024]{0:T(1024)}, u32[]{:S(2)}) copy-start(f32[1024]{0:T(1024)} %param.32) | copy-start | bytes 12292
  192.5 6.9 %copy-start.1 = (bf16[512,1024]{1,0:T(8,128)(2,1)S(1)}, bf16[512,1024]{1,0:T(8,128)(2,1)}, u32[]{:S(2)}) copy-start(bf16[512,1024]{1,0:T(8,128)(2,1)} %resid_ref.1) | copy-start | bytes 3145732
  192.6 6.9 %copy-start.2 = (bf16[16,4096]{1,0:T(8,128)(2,1)S(1)}, bf16[16,4096]{1,0:T(8,128)(2,1)}, u32[]{:S(2)}) copy-start(bf16[16,4096]{1,0:T(8,128)(2,1)} %down_ref.1) | copy-start | bytes 393220
  198.8 12.4 %copy-start.6 = (f32[1,4096]{1,0:T(1,128)}, f32[1,4096]{1,0:T(1,128)S(1)}, u32[]{:S(2)}) copy-start(f32[1,4096]{1,0:T(1,128)S(1)} %subtract_multiply_fusion) | copy-start | bytes 49156
  212.0 16.1 %all-to-all-start.2 = ((f32[4,24,512]{2,1,0:T(8,128)}), f32[4,24,512]{2,1,0:T(8,128)S(1)}, u32[]{:S(2)}, u32[]{:S(2)}) async-start(f32[4,24,512]{2,1,0:T(8,128)} %broadcast_in_dim.57), calls=%async_computation.2 | async-start | bytes 393216 | tf_op jit(solution)/shard_map/all_to_all | solution.py:34
  215.4 29.0 %copy-start.5 = (bf16[1,4096]{1,0:T(2,128)(2,1)S(1)}, bf16[1,4096]{1,0:T(2,128)(2,1)}, u32[]{:S(2)}) copy-start(bf16[1,4096]{1,0:T(2,128)(2,1)} %param.26) | copy-start | bytes 24580
  231.9 19.7 %all-to-all-start.3 = ((f32[16,1,2048]{2,1,0:T(1,128)}), f32[16,1,2048]{2,1,0:T(1,128)S(1)}, u32[]{:S(2)}, u32[]{:S(2)}) async-start(f32[16,1,2048]{2,1,0:T(1,128)} %reshape.288), calls=%async_computation.3 | async-start | bytes 262144 | tf_op jit(solution)/shard_map/all_to_all | solution.py:274
  254.1 13.2 %all-to-all-start.4 = ((f32[8,1,256]{2,1,0:T(1,128)}), f32[8,1,256]{2,1,0:T(1,128)S(1)}, u32[]{:S(2)}, u32[]{:S(2)}) async-start(f32[8,1,256]{2,1,0:T(1,128)} %reshape.290), calls=%async_computation.4 | async-start | bytes 16384 | tf_op jit(solution)/shard_map/all_to_all | solution.py:276
Sparse Core Ops, SparseCore 0:
  34.2 66.8 all-gather.1
